TPU v7x, 256 devices: a whole 4x4x8 slice. The times are simulated.
256 devices in a mesh: sec: 2 (over y_lo), tp: 8 (over y_hi, x), dp: 16 (over z, core).
Axes of the slice: x: 4, y: 4 (y_hi: 2, y_lo: 2; y = y_hi * 2 + y_lo), z: 8, core: 2. Of those that a mesh axis runs over, the one named last changes fastest.
Arguments:
- student_input: bfloat16 [2048, 4096], P('dp', ('sec', 'tp')), may hold values from -6 to 6
- teacher_hidden: bfloat16 [2048, 16384], P('dp', ('sec', 'tp')), may hold values from -10 to 10
- projector: bfloat16 [16384, 4096], P(('sec', 'tp'), 'dp'), may hold values from -0.0625 to 0.0625
- gate_weight: bfloat16 [7168, 4096], P(('sec', 'tp')), may hold values from -0.09375 to 0.09375
- up_weight: bfloat16 [7168, 4096], P(('sec', 'tp')), may hold values from -0.09375 to 0.09375
- down_weight: bfloat16 [7168, 4096], P(('sec', 'tp')), may hold values from -0.0625 to 0.0625
Outputs:
- distill_loss: float32 [], replicated
- grad_gate: float32 [7168, 4096], P(('sec', 'tp'), 'dp')
- grad_up: float32 [7168, 4096], P(('sec', 'tp'), 'dp')
- grad_down: float32 [7168, 4096], P(('sec', 'tp'), 'dp')
All inputs are finite; a program needn't handle non-finite values.
Results may differ from a plain program's by a relative error of at most 0.0041.
Values may be sent and summed in bfloat16 or wider, within the bound.
No kernel may reach another device: no remote copies, remote signals or barrier semaphores. Data moves between devices by JAX's collectives and lax.ppermute only.
A program may use at most 128 MiB of HBM per device.

v0:
```python
import functools

import jax
import jax.numpy as jnp
from jax import lax
from jax.experimental import pallas as pl
from jax.experimental.pallas import tpu as pltpu
from jax.sharding import PartitionSpec as P

epsilon = 1e-05

GROUP = ("sec", "tp")
EVERY = ("sec", "tp", "dp")
LINES = [[2 * z + c for z in range(8)] for c in range(2)]
SIBLING = [(d, d ^ 1) for d in range(16)]
SWAP = [
    (s * 16 + d, ((d & 14) | (s & 1)) * 16 + ((s & 14) | (d & 1)))
    for s in range(16)
    for d in range(16)
]


def silu_parts(gate_val):
    sigma = jax.nn.sigmoid(gate_val)
    return (gate_val * sigma, sigma * (1.0 + gate_val * (1.0 - sigma)))


def contract_cols(left, right):
    return lax.dot_general(
        left, right, (((1,), (1,)), ((), ())), preferred_element_type=jnp.float32
    )


def gather_group(block):
    copies = jnp.broadcast_to(block[None], (16,) + block.shape)
    return lax.all_to_all(copies, GROUP, 0, 0, tiled=True)


RIGHT = [(d, (d + 2) % 16) for d in range(16)]
LEFT = [(d, (d - 2) % 16) for d in range(16)]


def ring(block):
    half = block.shape[0] // 2
    up = down = block
    found = [[(0, block)]] + [[] for _ in range(7)]
    for step in range(1, 4):
        up, down = lax.ppermute(up, "dp", RIGHT), lax.ppermute(down, "dp", LEFT)
        found[-step], found[step] = [(0, up)], [(0, down)]
    up, down = lax.ppermute(up[:half], "dp", RIGHT), lax.ppermute(down[half:], "dp", LEFT)
    found[4] = [(0, up), (half, down)]
    return found


def fetch(pairs, sems):
    copies = [pltpu.make_async_copy(src, dst, sems.at[i]) for i, (src, dst) in enumerate(pairs)]
    for copy in copies:
        copy.start()
    return copies


def down_kernel(place_ref, hidden_ref, down_ref, out_ref):
    width = out_ref.shape[2]
    for i in range(8):
        columns = pl.ds(pl.multiple_of((2 * i + place_ref[1]) * width, width), width)
        out_ref[i] = lax.dot_general(
            hidden_ref[...],
            down_ref[:, columns],
            (((0,), (0,)), ((), ())),
            preferred_element_type=jnp.float32,
        )


def split_rows(value, count):
    high = value.astype(jnp.bfloat16).astype(jnp.float32)
    mid = (value - high).astype(jnp.bfloat16).astype(jnp.float32)
    shape = (count, value.shape[1])
    row = lax.broadcasted_iota(jnp.int32, shape, 0)
    rows = jnp.zeros(shape, jnp.float32)
    for i, part in enumerate((high, mid, value - high - mid)):
        rows = jnp.where(row == i, jnp.broadcast_to(part, shape), rows)
    return rows.astype(jnp.bfloat16)


def mismatch_kernel(tokens_all, blocks_ref, inputs_ref, copies_ref, outgrad_ref):
    tokens = inputs_ref.shape[0]
    mismatch = blocks_ref[0].astype(jnp.float32)
    for i in range(1, 16):
        mismatch = mismatch + blocks_ref[i].astype(jnp.float32)
    mismatch = inputs_ref[...].astype(jnp.float32) + mismatch
    loss = jnp.sum(mismatch * mismatch, axis=0, keepdims=True)
    loss = split_rows(loss[:, :tokens] + loss[:, tokens:], 16)
    loss = jnp.concatenate([loss, jnp.zeros_like(loss)], axis=1)
    outgrad = (mismatch * (1.0 / tokens_all)).astype(jnp.bfloat16)
    outgrad_ref[...] = outgrad
    for i in range(16):
        copies_ref[i, :tokens] = outgrad
        copies_ref[i, tokens:] = loss


def hidden_kernel(tokens, blocks_ref, down_ref, out_ref):
    width = blocks_ref.shape[2]
    units = down_ref.shape[0]
    total = loss = None
    for i in range(16):
        found = contract_cols(down_ref[:, i * width : (i + 1) * width], blocks_ref[i, :tokens])
        total = found if total is None else total + found
        rows = blocks_ref[i, tokens : tokens + 16, :tokens].astype(jnp.float32)
        loss = rows if loss is None else loss + rows
    out_ref[:units] = total.astype(out_ref.dtype)
    loss = jnp.sum(loss, axis=0, keepdims=True)
    out_ref[units:] = split_rows(loss, out_ref.shape[0] - units)


def columns_of(ref, half, start):
    return jnp.concatenate(
        [ref[2 * lax.rem(start + i, 8) + half] for i in range(8)], axis=0
    )


def grads_kernel(tokens, spans, place_ref, gates_hbm, inputs_hbm, outgrads_hbm, *refs):
    count = sum(len(span) for span in spans)
    blocks, theirs_refs, mine_ref = refs[:count], refs[count : count + 3], refs[count + 3]
    gates_ref, inputs_ref, outgrads_ref, block_ref, lefts_ref, sems = refs[count + 4 :]
    start, core = place_ref[0], place_ref[1]
    units = lefts_ref.shape[1]
    spots = [lax.rem(start + i, 8) for i in range(8)]
    pieces = iter(blocks)
    pairs = []
    for i, span in enumerate(spans):
        pairs.append((gates_hbm.at[spots[i]], gates_ref.at[i]))
        for first, rows in span:
            source = next(pieces).at[pl.ds(0, rows)]
            pairs.append((source, block_ref.at[i, pl.ds(first, rows)]))
    pairs += [(inputs_hbm, inputs_ref), (outgrads_hbm, outgrads_ref)]
    waiting = iter(fetch(pairs, sems))
    for i in range(8):
        for _ in range(1 + len(spans[i])):
            next(waiting).wait()
        columns = pl.ds(i * tokens, tokens)
        gate, up = gates_ref[i, :units], gates_ref[i, units:]
        grad_hidden = block_ref[i].astype(jnp.float32)
        activated, slope = silu_parts(gate)
        lefts_ref[0, :, columns] = (grad_hidden * up * slope).astype(jnp.bfloat16)
        lefts_ref[1, :, columns] = (grad_hidden * activated).astype(jnp.bfloat16)
        lefts_ref[2, :, columns] = (activated * up).astype(jnp.bfloat16)
    for copy in waiting:
        copy.wait()
    for mine, half in ((False, 1 - core), (True, core)):
        inputs = columns_of(inputs_ref, half, start)
        outgrads = columns_of(outgrads_ref, half, start)
        for part, right in enumerate((inputs, inputs, outgrads)):
            found = jnp.dot(lefts_ref[part], right, preferred_element_type=jnp.float32)
            if mine:
                mine_ref[part] = found
            else:
                theirs_refs[part][...] = found


def scatter_sum(parts):
    return jnp.sum(
        lax.all_to_all(parts, GROUP, 0, 0, tiled=True).astype(jnp.float32), axis=0
    )


def split3(value):
    high = lax.reduce_precision(value, 8, 7)
    mid = lax.reduce_precision(value - high, 8, 7)
    low = value - high - mid
    return jnp.stack([high, mid, low]).astype(jnp.bfloat16)


def with_rows(block, extra):
    columns = block.shape[1]
    rows = jnp.pad(split3(extra), ((0, 13), (0, columns - extra.shape[0])))
    return jnp.concatenate([block, rows], axis=0)


def rows_of(blocks, tokens, count):
    rows = blocks[:, tokens : tokens + 3, :count].astype(jnp.float32)
    return jnp.sum(jnp.sum(rows, axis=1), axis=0)


def shards(student_input, teacher_hidden, projector, gate_weight, up_weight, down_weight):
    tokens, width = student_input.shape
    units = gate_weight.shape[0]
    tokens_all = tokens * 16
    teacher_units = teacher_hidden.shape[1] * 16
    place = lax.axis_index("dp")
    core = lax.rem(place, 2)
    start = lax.div(place, 2)
    where = jnp.stack([start, core])
    vmem, anywhere = pl.BlockSpec(memory_space=pltpu.VMEM), pl.BlockSpec(memory_space=pl.ANY)
    smem = pl.BlockSpec(memory_space=pltpu.SMEM)

    projector_line = lax.all_gather(projector, "dp", axis=0, axis_index_groups=LINES)
    inputs_moved = lax.ppermute(student_input, EVERY, SWAP)
    teacher_pair = jnp.concatenate(
        [teacher_hidden, lax.ppermute(teacher_hidden, "dp", SIBLING)], axis=0
    )
    teacher_float = teacher_hidden.astype(jnp.float32)
    squares = jnp.sum(teacher_float * teacher_float, axis=1)

    gathered = gather_group(with_rows(student_input, squares))
    inputs_moved, _ = lax.optimization_barrier((inputs_moved, gathered))
    inputs_swapped = gather_group(inputs_moved)
    row_total = rows_of(gathered, tokens, tokens)
    row_scale = 1.0 / jnp.sqrt(row_total / teacher_units + epsilon)
    scale_pair = jnp.concatenate([row_scale, lax.ppermute(row_scale, "dp", SIBLING)])[:, None]
    inputs_full = gathered[:, :tokens].transpose(1, 0, 2).reshape(tokens, 16 * width)

    gate_val = contract_cols(gate_weight, inputs_full)
    up_val = contract_cols(up_weight, inputs_full)
    hidden = (silu_parts(gate_val)[0] * up_val).astype(jnp.bfloat16)
    hidden_pair = jnp.concatenate([hidden, lax.ppermute(hidden, "dp", SIBLING)], axis=1)

    down_part = pl.pallas_call(
        down_kernel,
        out_shape=jax.ShapeDtypeStruct((8, 2 * tokens, width), jnp.float32),
        in_specs=[smem, vmem, vmem],
        out_specs=vmem,
        compiler_params=pltpu.CompilerParams(vmem_limit_bytes=16 * 2**20),
        cost_estimate=pl.CostEstimate(
            flops=2 * 256 * 448 * 2048, bytes_accessed=6 * 2**20, transcendentals=0
        ),
    )(where, hidden_pair, down_weight)
    projected = jnp.einsum(
        "tk,zkn->ztn",
        teacher_pair,
        projector_line,
        preferred_element_type=jnp.float32,
    )
    part = (down_part - projected * scale_pair).astype(jnp.bfloat16)
    mine, other = part[:, :tokens], part[:, tokens:]
    other = lax.ppermute(other, "dp", SIBLING)
    parts = jnp.stack(
        [jnp.where(core == 0, mine, other), jnp.where(core == 0, other, mine)], axis=1
    ).reshape(16, tokens, width)
    gates = jnp.concatenate([gate_val, up_val], axis=0)
    gates, parts, inputs_swapped = lax.optimization_barrier((gates, parts, inputs_swapped))
    gates_line = lax.all_gather(gates, "dp", axis=0, axis_index_groups=LINES)
    blocks = lax.all_to_all(parts, GROUP, 0, 0, tiled=True)
    copies, outgrad_part = pl.pallas_call(
        functools.partial(mismatch_kernel, tokens_all),
        out_shape=(
            jax.ShapeDtypeStruct((16, tokens + 16, width), jnp.bfloat16),
            jax.ShapeDtypeStruct((tokens, width), jnp.bfloat16),
        ),
        in_specs=[vmem, vmem],
        out_specs=(vmem, vmem),
        compiler_params=pltpu.CompilerParams(vmem_limit_bytes=16 * 2**20),
        cost_estimate=pl.CostEstimate(
            flops=2**20, bytes_accessed=3 * 2**20, transcendentals=0
        ),
    )(blocks, student_input)
    outgrad_gathered = lax.all_to_all(copies, GROUP, 0, 0, tiled=True)
    outgrad_moved = lax.ppermute(outgrad_part, EVERY, SWAP)

    grad_hidden = pl.pallas_call(
        functools.partial(hidden_kernel, tokens),
        out_shape=jax.ShapeDtypeStruct((units + 32, tokens), jnp.bfloat16),
        in_specs=[vmem, vmem],
        out_specs=vmem,
        compiler_params=pltpu.CompilerParams(vmem_limit_bytes=16 * 2**20),
        cost_estimate=pl.CostEstimate(
            flops=2 * 128 * 448 * 4096, bytes_accessed=5 * 2**20, transcendentals=0
        ),
    )(outgrad_gathered, down_weight)
    outgrad_moved, _ = lax.optimization_barrier((outgrad_moved, grad_hidden))
    outgrad_swapped = gather_group(outgrad_moved)
    line = ring(grad_hidden)
    line_loss = jnp.stack([found[-1][1][units - found[-1][0] :] for found in line])
    line_loss = rows_of(line_loss, 0, tokens)
    spans = [[(first, min(piece.shape[0], units - first)) for first, piece in found] for found in line]
    pieces = [piece for found in line for _, piece in found]

    grad = jax.ShapeDtypeStruct((units, width), jnp.float32)
    *theirs, mine = pl.pallas_call(
        functools.partial(grads_kernel, tokens, spans),
        out_shape=(grad, grad, grad, jax.ShapeDtypeStruct((3, units, width), jnp.float32)),
        in_specs=[smem] + [anywhere] * (3 + len(pieces)),
        out_specs=(vmem,) * 4,
        scratch_shapes=[
            pltpu.VMEM(gates_line.shape, jnp.float32),
            pltpu.VMEM(inputs_swapped.shape, jnp.bfloat16),
            pltpu.VMEM(outgrad_swapped.shape, jnp.bfloat16),
            pltpu.VMEM((8, units, tokens), jnp.bfloat16),
            pltpu.VMEM((3, units, 8 * tokens), jnp.bfloat16),
            pltpu.SemaphoreType.DMA((10 + len(pieces),)),
        ],
        compiler_params=pltpu.CompilerParams(vmem_limit_bytes=60 * 2**20),
        cost_estimate=pl.CostEstimate(
            flops=2 * 3 * 1024 * 448 * 512, bytes_accessed=10 * 2**20, transcendentals=2**19
        ),
    )(where, gates_line, inputs_swapped, outgrad_swapped, *pieces)
    theirs = [lax.ppermute(part, "dp", SIBLING) for part in theirs]
    grad_gate, grad_up, grad_down = [mine[part] + theirs[part] for part in range(3)]
    all_loss = line_loss + lax.ppermute(line_loss, "dp", SIBLING)
    loss_value = 0.5 * jnp.sum(all_loss) / tokens_all
    return (loss_value, grad_gate, grad_up, grad_down)


def solution(mesh):
    in_specs = (
        P("dp", ("sec", "tp")),
        P("dp", ("sec", "tp")),
        P(("sec", "tp"), "dp"),
        P(("sec", "tp"), None),
        P(("sec", "tp"), None),
        P(("sec", "tp"), None),
    )
    out_specs = (P(), P(("sec", "tp"), "dp"), P(("sec", "tp"), "dp"), P(("sec", "tp"), "dp"))
    return jax.shard_map(shards, mesh=mesh, in_specs=in_specs, out_specs=out_specs, check_vma=False)
```

profile of v0, /device:TPU:1, one launch (start us, length us, event | category | flops | bytes accessed | tf_op | source)
XLA Modules:
  0.0 182.2 jit_solution(805231242635918602)
XLA Ops:
  7.2 0.7 all-gather.5.cloned.1.call-update
  7.9 1.1 multiply_reduce_fusion
  9.1 0.8 pad_maximum_fusion.3
  9.9 1.1 broadcast_in_dim.6
  11.0 7.6 %all-to-all-start = ((bf16[16,144,256]{2,1,0:T(8,128)(2,1)}), bf16[16,144,256]{2,1,0:T(8,128)(2,1)S(1)}, u32[]{:S(2)}, u32[]{:S(2)}) async-start(bf16[16,144,256]{2,1,0:T(8,128)(2,1)} %broadcast_in_dim.6), calls=%async_computation | async-start | bytes 2359296 | tf_op jit(solution)/shard_map/all_to_all | solution.py:36
  18.6 0.7 collective-permute-start.4
  19.3 1.0 collective-permute-start.1
  20.4 16.5 %all-to-all-done = bf16[16,144,256]{2,1,0:T(8,128)(2,1)S(1)} async-done(((bf16[16,144,256]{2,1,0:T(8,128)(2,1)}), bf16[16,144,256]{2,1,0:T(8,128)(2,1)S(1)}, u32[]{:S(2)}, u32[]{:S(2)}) %all-to-all-start) | async-done | bytes 1179680 | tf_op jit(solution)/shard_map/all_to_all | solution.py:36
  37.0 0.7 copy.15
  37.7 2.6 %collective-permute-start.2 = (f32[128]{0:T(128)S(1)}, f32[128]{0:T(128)S(1)}, u32[]{:S(2)}, u32[]{:S(2)}) collective-permute-start(f32[128]{0:T(128)S(1)} %add_rsqrt_fusion), channel_id=1, source_target_pairs={{0,1},{1,0},{2,3},{3,2},{4,5},{5,4},{6,7},{7,6},{8,9},{9,8},{10,11... | collective-permute-start | bytes 1544 | tf_op jit(solution)/shard_map/ppermute | solution.py:209
  40.3 3.3 %convolution_bitcast_fusion.1 = f32[448,128]{1,0:T(8,128)S(1)} fusion(bf16[448,4096]{1,0:T(8,128)(2,1)} %param.9, bf16[128,4096]{0,1:T(8,128)(2,1)S(1)} %bitcast.74), kind=kOutput, calls=%fused_computation.3 | convolution fusion | flops 469762048 | bytes 4947968 | tf_op jit(solution)/shard_map/dot_general | solution.py:29
  43.6 1.8 multiply_convert_fusion
  45.5 1.1 broadcast_in_dim.7
  46.6 5.0 %all-to-all-start.1 = ((bf16[16,128,256]{2,1,0:T(8,128)(2,1)}), bf16[16,128,256]{2,1,0:T(8,128)(2,1)}, u32[]{:S(2)}, u32[]{:S(2)}) async-start(bf16[16,128,256]{2,1,0:T(8,128)(2,1)} %broadcast_in_dim.7), calls=%async_computation.1 | async-start | bytes 2097152 | tf_op jit(solution)/shard_map/all_to_all | solution.py:36
  51.8 2.1 %copy-done = bf16[448,4096]{1,0:T(8,128)(2,1)S(1)} copy-done((bf16[448,4096]{1,0:T(8,128)(2,1)S(1)}, bf16[448,4096]{1,0:T(8,128)(2,1)}, u32[]{:S(2)}) %copy-start) | copy-done | bytes 3670040
  53.9 1.3 shard_map.93
  55.2 18.3 %all-gather.5.cloned.1.call-done = bf16[8192,256]{1,0:T(8,128)(2,1)} async-done(((bf16[1024,256]{1,0:T(8,128)(2,1)}), bf16[8192,256]{1,0:T(8,128)(2,1)}) %all-gather.5.cloned.1.call-update) | async-done | bytes 4194320 | tf_op jit(solution)/shard_map/all_gather | solution.py:196
  73.5 3.6 %fusion.1 = f32[256,8,256]{2,0,1:T(8,128)S(1)} fusion(bf16[8,1024,256]{2,1,0:T(8,128)(2,1)} %bitcast.77, bf16[128,1024]{1,0:T(8,128)(2,1)} %collective-permute-done.1, bf16[128,1024]{1,0:T(8,128)(2,1)} %param.7), kind=kOutput, calls=%fused_computation.6 | convolution fusion | flops 1074790400 | bytes 6815744 | tf_op jit(solution)/shard_map/tk,zkn->ztn/dot_general | solution.py:227
  77.5 0.5 collective-permute-start.3
  78.1 1.7 pad_maximum_fusion.1
  80.1 20.0 %all_to_all.25.blocks_ref = bf16[16,128,256]{2,1,0:T(8,128)(2,1)S(1)} all-to-all(bf16[16,128,256]{2,1,0:T(8,128)(2,1)S(1)} %bitcast.73), channel_id=1, replica_groups=mesh['sec'=2,'tp'=8,'dp'=16] {'sec','tp'}, dimensions={0} | all-to-all | bytes 2097152 | tf_op jit(solution)/shard_map/all_to_all | solution.py:242
  100.1 1.2 shard_map.94
  101.3 3.7 %all-to-all-start.3 = ((bf16[16,144,256]{2,1,0:T(8,128)(2,1)}), bf16[16,144,256]{2,1,0:T(8,128)(2,1)S(1)}, u32[]{:S(2)}, u32[]{:S(2)}) async-start(bf16[16,144,256]{2,1,0:T(8,128)(2,1)} %get-tuple-element.17), calls=%async_computation.3 | async-start | bytes 2359296 | tf_op jit(solution)/shard_map/all_to_all | solution.py:256
  105.0 0.7 collective-permute-start.13
  105.7 17.0 %all-to-all-done.3.blocks_ref = bf16[16,144,256]{2,1,0:T(8,128)(2,1)S(1)} async-done(((bf16[16,144,256]{2,1,0:T(8,128)(2,1)}), bf16[16,144,256]{2,1,0:T(8,128)(2,1)S(1)}, u32[]{:S(2)}, u32[]{:S(2)}) %all-to-all-start.3) | async-done | bytes 1179680 | tf_op jit(solution)/shard_map/all_to_all | solution.py:256
  122.7 2.1 %copy-done.1 = bf16[448,4096]{1,0:T(8,128)(2,1)S(1)} copy-done((bf16[448,4096]{1,0:T(8,128)(2,1)S(1)}, bf16[448,4096]{1,0:T(8,128)(2,1)}, u32[]{:S(2)}) %copy-start.1) | copy-done | bytes 3670040
  124.8 1.1 shard_map.95.refs_0_
  125.9 3.7 %collective-permute-start.9 = (bf16[480,128]{1,0:T(8,128)(2,1)S(1)}, bf16[480,128]{1,0:T(8,128)(2,1)S(1)}, u32[]{:S(2)}, u32[]{:S(2)}) collective-permute-start(bf16[480,128]{1,0:T(8,128)(2,1)S(1)} %shard_map.95.refs_0_), channel_id=1, source_target_pairs={{0,2},{1,3},{2,4},{3,5},{4,6},{5,7},{6,8},{7,9},{8,10},{9,11},{10,... | collective-permute-start | bytes 368648 | tf_op jit(solution)/shard_map/ppermute | solution.py:48
  129.6 3.8 %collective-permute-start.5 = (bf16[480,128]{1,0:T(8,128)(2,1)S(1)}, bf16[480,128]{1,0:T(8,128)(2,1)S(1)}, u32[]{:S(2)}, u32[]{:S(2)}) collective-permute-start(bf16[480,128]{1,0:T(8,128)(2,1)S(1)} %shard_map.95.refs_0_), channel_id=1, source_target_pairs={{0,14},{1,15},{2,0},{3,1},{4,2},{5,3},{6,4},{7,5},{8,6},{9,7},{10,... | collective-permute-start | bytes 368648 | tf_op jit(solution)/shard_map/ppermute | solution.py:48
  133.5 1.1 broadcast_in_dim.8
  134.5 3.7 %all-to-all-start.4 = ((bf16[16,128,256]{2,1,0:T(8,128)(2,1)}), bf16[16,128,256]{2,1,0:T(8,128)(2,1)S(1)}, u32[]{:S(2)}, u32[]{:S(2)}) async-start(bf16[16,128,256]{2,1,0:T(8,128)(2,1)} %broadcast_in_dim.8), calls=%async_computation.4 | async-start | bytes 2097152 | tf_op jit(solution)/shard_map/all_to_all | solution.py:36
  138.3 2.6 %collective-permute-start.6 = (bf16[480,128]{1,0:T(8,128)(2,1)S(1)}, bf16[480,128]{1,0:T(8,128)(2,1)S(1)}, u32[]{:S(2)}, u32[]{:S(2)}) collective-permute-start(bf16[480,128]{1,0:T(8,128)(2,1)S(1)} %collective-permute-done.5.refs_1_), channel_id=1, source_target_pairs={{0,14},{1,15},{2,0},{3,1},{4,2},{5,3},{6,4},{7,5},{8,6},{9,7},{10,... | collective-permute-start | bytes 368648 | tf_op jit(solution)/shard_map/ppermute | solution.py:48
  141.0 2.2 %collective-permute-done.10.refs_7_ = bf16[480,128]{1,0:T(8,128)(2,1)S(1)} collective-permute-done((bf16[480,128]{1,0:T(8,128)(2,1)S(1)}, bf16[480,128]{1,0:T(8,128)(2,1)S(1)}, u32[]{:S(2)}, u32[]{:S(2)}) %collective-permute-start.10) | collective-permute-done | bytes 122912 | tf_op jit(solution)/shard_map/ppermute | solution.py:48
  143.3 2.7 %collective-permute-start.7 = (bf16[480,128]{1,0:T(8,128)(2,1)S(1)}, bf16[480,128]{1,0:T(8,128)(2,1)S(1)}, u32[]{:S(2)}, u32[]{:S(2)}) collective-permute-start(bf16[480,128]{1,0:T(8,128)(2,1)S(1)} %collective-permute-done.6.refs_2_), channel_id=1, source_target_pairs={{0,14},{1,15},{2,0},{3,1},{4,2},{5,3},{6,4},{7,5},{8,6},{9,7},{10,... | collective-permute-start | bytes 368648 | tf_op jit(solution)/shard_map/ppermute | solution.py:48
  145.9 2.5 %collective-permute-done.11.refs_6_ = bf16[480,128]{1,0:T(8,128)(2,1)S(1)} collective-permute-done((bf16[480,128]{1,0:T(8,128)(2,1)S(1)}, bf16[480,128]{1,0:T(8,128)(2,1)S(1)}, u32[]{:S(2)}, u32[]{:S(2)}) %collective-permute-start.11) | collective-permute-done | bytes 122912 | tf_op jit(solution)/shard_map/ppermute | solution.py:48
  148.6 2.8 %collective-permute-start.8 = (bf16[240,128]{1,0:T(8,128)(2,1)S(1)}, bf16[240,128]{1,0:T(8,128)(2,1)S(1)}, u32[]{:S(2)}, u32[]{:S(2)}) collective-permute-start(bf16[240,128]{1,0:T(8,128)(2,1)S(1)} %slice.80), channel_id=1, source_target_pairs={{0,14},{1,15},{2,0},{3,1},{4,2},{5,3},{6,4},{7,5},{8,6},{9,7},{10,... | collective-permute-start | bytes 184328 | tf_op jit(solution)/shard_map/ppermute | solution.py:50
  151.5 1.8 collective-permute-done.8.refs_5_
  153.3 0.4 collective-permute-done.14.refs_4_
  153.9 0.5 copy-done.15
  154.4 0.4 copy-done.5
  154.7 6.5 %shard_map.96 = (f32[448,256]{1,0:T(8,128)}, f32[448,256]{1,0:T(8,128)}, f32[448,256]{1,0:T(8,128)}, f32[3,448,256]{2,1,0:T(8,128)}) custom-call(s32[2]{0:T(128)} %copy-done.4, f32[8,896,128]{2,1,0:T(8,128)} %bitcast.76, bf16[16,128,256]{2,1,0:T(8,128)(2,1)} %all-to-all-done.1.inputs_hbm, bf16[16,128,256]{2,1,0:T(8,128)(2,1)} %copy-done.5, ...), custom_call_target="tpu_custom_call" | custom-call | flops 1409286144 | bytes 10485760 | tf_op jit(solution)/shard_map/pallas_call | solution.py:278
  161.2 6.1 %collective-permute-start.15 = (f32[448,256]{1,0:T(8,128)}, f32[448,256]{1,0:T(8,128)S(1)}, u32[]{:S(2)}, u32[]{:S(2)}) collective-permute-start(f32[448,256]{1,0:T(8,128)} %get-tuple-element.23), channel_id=1, source_target_pairs={{0,1},{1,0},{2,3},{3,2},{4,5},{5,4},{6,7},{7,6},{8,9},{9,8},{10,11... | collective-permute-start | bytes 1376264 | tf_op jit(solution)/shard_map/ppermute | solution.py:296
  167.4 0.4 collective-permute-start.17
  167.8 0.7 constant_dynamic-update-slice_fusion.1
  168.6 0.7 constant_dynamic-update-slice_fusion
  169.5 1.0 collective-permute-done.12
  170.5 0.6 add_reduce_fusion
  171.8 2.4 %bitcast_add_fusion = (f32[448,256]{1,0:T(8,128)}, f32[448,256]{1,0:T(8,128)}, f32[448,256]{1,0:T(8,128)}) fusion(f32[448,256]{1,0:T(8,128)S(1)} %collective-permute-done.17, f32[3,448,256]{2,1,0:T(8,128)} %get-tuple-element.22, f32[448,256]{1,0:T(8,128)S(1)} %collective-permute-done.16, f32[448,256]{1,0:T(8,128)S(1)} %collective-permute-done.15), kind=kLoop, calls=%fused_computation.13 | loop fusion | flops 344064 | bytes 4128768 | tf_op jit(solution)/shard_map/add | solution.py:297
  (77 shorter events, 1.7 us)
Async XLA Ops:
  7.2 66.4 %all-gather.5.cloned.1.call-start = ((), (), s32[]{:S(2)}) async-start(), calls=%async_computation.5 | async-start | bytes 4718592 | tf_op jit(solution)/shard_map/all_gather | solution.py:196
  7.9 10.7 %copy-start.3 = (bf16[128,256]{1,0:T(8,128)(2,1)S(1)}, bf16[128,256]{1,0:T(8,128)(2,1)}, u32[]{:S(2)}) copy-start(bf16[128,256]{1,0:T(8,128)(2,1)} %inputs_ref.1) | copy-start | bytes 196612
  11.0 25.8 %all-to-all-start = ((bf16[16,144,256]{2,1,0:T(8,128)(2,1)}), bf16[16,144,256]{2,1,0:T(8,128)(2,1)S(1)}, u32[]{:S(2)}, u32[]{:S(2)}) async-start(bf16[16,144,256]{2,1,0:T(8,128)(2,1)} %broadcast_in_dim.6), calls=%async_computation | async-start | bytes 2359296 | tf_op jit(solution)/shard_map/all_to_all | solution.py:36
  18.6 26.9 %collective-permute-start.4 = (bf16[128,256]{1,0:T(8,128)(2,1)S(1)}, bf16[128,256]{1,0:T(8,128)(2,1)S(1)}, u32[]{:S(2)}, u32[]{:S(2)}) collective-permute-start(bf16[128,256]{1,0:T(8,128)(2,1)S(1)} %copy-done.3), channel_id=1, source_target_pairs={{0,0},{1,1},{2,32},{3,33},{4,64},{5,65},{6,96},{7,97},{8,128},{9,1... | collective-permute-start | bytes 196616 | tf_op jit(solution)/shard_map/ppermute | solution.py:197
  19.3 35.9 %collective-permute-start.1 = (bf16[128,1024]{1,0:T(8,128)(2,1)}, bf16[128,1024]{1,0:T(8,128)(2,1)}, u32[]{:S(2)}, u32[]{:S(2)}) collective-permute-start(bf16[128,1024]{1,0:T(8,128)(2,1)} %param.7), channel_id=1, source_target_pairs={{0,1},{1,0},{2,3},{3,2},{4,5},{5,4},{6,7},{7,6},{8,9},{9,8},{10,11... | collective-permute-start | bytes 786440 | tf_op jit(solution)/shard_map/ppermute | solution.py:199
  37.7 14.0 %collective-permute-start.2 = (f32[128]{0:T(128)S(1)}, f32[128]{0:T(128)S(1)}, u32[]{:S(2)}, u32[]{:S(2)}) collective-permute-start(f32[128]{0:T(128)S(1)} %add_rsqrt_fusion), channel_id=1, source_target_pairs={{0,1},{1,0},{2,3},{3,2},{4,5},{5,4},{6,7},{7,6},{8,9},{9,8},{10,11... | collective-permute-start | bytes 1544 | tf_op jit(solution)/shard_map/ppermute | solution.py:209
  40.3 3.3 %copy-start.16 = (bf16[448,4096]{1,0:T(8,128)(2,1)S(1)}, bf16[448,4096]{1,0:T(8,128)(2,1)}, u32[]{:S(2)}) copy-start(bf16[448,4096]{1,0:T(8,128)(2,1)} %param.10) | copy-start | bytes 11010052
  43.6 1.8 %copy-start.6 = (f32[448,128]{1,0:T(8,128)}, f32[448,128]{1,0:T(8,128)S(1)}, u32[]{:S(2)}) copy-start(f32[448,128]{1,0:T(8,128)S(1)} %convolution_bitcast_fusion.1) | copy-start | bytes 688132
  45.4 6.3 %collective-permute-start = (bf16[448,128]{1,0:T(8,128)(2,1)S(1)}, bf16[448,128]{1,0:T(8,128)(2,1)S(1)}, u32[]{:S(2)}, u32[]{:S(2)}) collective-permute-start(bf16[448,128]{1,0:T(8,128)(2,1)S(1)} %get-tuple-element.34), channel_id=1, source_target_pairs={{0,1},{1,0},{2,3},{3,2},{4,5},{5,4},{6,7},{7,6},{8,9},{9,8},{10,11... | collective-permute-start | bytes 344072 | tf_op jit(solution)/shard_map/ppermute | solution.py:215
  45.5 9.6 %copy-start.4 = (s32[2]{0:T(128)}, s32[2]{0:T(128)S(1)}, u32[]{:S(2)}) copy-start(s32[2]{0:T(128)S(1)} %pad_add_fusion.place_ref) | copy-start | bytes 28
  46.6 33.5 %all-to-all-start.1 = ((bf16[16,128,256]{2,1,0:T(8,128)(2,1)}), bf16[16,128,256]{2,1,0:T(8,128)(2,1)}, u32[]{:S(2)}, u32[]{:S(2)}) async-start(bf16[16,128,256]{2,1,0:T(8,128)(2,1)} %broadcast_in_dim.7), calls=%async_computation.1 | async-start | bytes 2097152 | tf_op jit(solution)/shard_map/all_to_all | solution.py:36
  51.6 102.1 %all-gather.7.cloned.1.call-start = ((), (), s32[]{:S(2)}) async-start(), calls=%async_computation.6 | async-start | bytes 4128768 | tf_op jit(solution)/shard_map/all_gather | solution.py:241
  51.8 2.1 %copy-start = (bf16[448,4096]{1,0:T(8,128)(2,1)S(1)}, bf16[448,4096]{1,0:T(8,128)(2,1)}, u32[]{:S(2)}) copy-start(bf16[448,4096]{1,0:T(8,128)(2,1)} %down_ref.3) | copy-start | bytes 11010052
  77.1 0.9 copy-start.7
  77.5 2.3 %collective-permute-start.3 = (bf16[8,128,256]{2,1,0:T(8,128)(2,1)S(1)}, bf16[8,128,256]{2,1,0:T(8,128)(2,1)S(1)}, u32[]{:S(2)}, u32[]{:S(2)}) collective-permute-start(bf16[8,128,256]{2,1,0:T(8,128)(2,1)S(1)} %slice.75), channel_id=1, source_target_pairs={{0,1},{1,0},{2,3},{3,2},{4,5},{5,4},{6,7},{7,6},{8,9},{9,8},{10,11... | collective-permute-start | bytes 1572872 | tf_op jit(solution)/shard_map/ppermute | solution.py:235
  101.3 21.4 %all-to-all-start.3 = ((bf16[16,144,256]{2,1,0:T(8,128)(2,1)}), bf16[16,144,256]{2,1,0:T(8,128)(2,1)S(1)}, u32[]{:S(2)}, u32[]{:S(2)}) async-start(bf16[16,144,256]{2,1,0:T(8,128)(2,1)} %get-tuple-element.17), calls=%async_computation.3 | async-start | bytes 2359296 | tf_op jit(solution)/shard_map/all_to_all | solution.py:256
  105.0 28.4 %collective-permute-start.13 = (bf16[128,256]{1,0:T(8,128)(2,1)S(1)}, bf16[128,256]{1,0:T(8,128)(2,1)S(1)}, u32[]{:S(2)}, u32[]{:S(2)}) collective-permute-start(bf16[128,256]{1,0:T(8,128)(2,1)S(1)} %get-tuple-element.20), channel_id=1, source_target_pairs={{0,0},{1,1},{2,32},{3,33},{4,64},{5,65},{6,96},{7,97},{8,128},{9,1... | collective-permute-start | bytes 196616 | tf_op jit(solution)/shard_map/ppermute | solution.py:257
  122.7 2.1 %copy-start.1 = (bf16[448,4096]{1,0:T(8,128)(2,1)S(1)}, bf16[448,4096]{1,0:T(8,128)(2,1)}, u32[]{:S(2)}) copy-start(bf16[448,4096]{1,0:T(8,128)(2,1)} %down_ref.3) | copy-start | bytes 11010052
  125.9 27.9 %copy-start.2 = (bf16[480,128]{1,0:T(8,128)(2,1)}, bf16[480,128]{1,0:T(8,128)(2,1)S(1)}, u32[]{:S(2)}) copy-start(bf16[480,128]{1,0:T(8,128)(2,1)S(1)} %shard_map.95.refs_0_) | copy-start | bytes 368644
  125.9 12.3 %collective-permute-start.9 = (bf16[480,128]{1,0:T(8,128)(2,1)S(1)}, bf16[480,128]{1,0:T(8,128)(2,1)S(1)}, u32[]{:S(2)}, u32[]{:S(2)}) collective-permute-start(bf16[480,128]{1,0:T(8,128)(2,1)S(1)} %shard_map.95.refs_0_), channel_id=1, source_target_pairs={{0,2},{1,3},{2,4},{3,5},{4,6},{5,7},{6,8},{7,9},{8,10},{9,11},{10,... | collective-permute-start | bytes 368648 | tf_op jit(solution)/shard_map/ppermute | solution.py:48
  129.6 8.7 %collective-permute-start.5 = (bf16[480,128]{1,0:T(8,128)(2,1)S(1)}, bf16[480,128]{1,0:T(8,128)(2,1)S(1)}, u32[]{:S(2)}, u32[]{:S(2)}) collective-permute-start(bf16[480,128]{1,0:T(8,128)(2,1)S(1)} %shard_map.95.refs_0_), channel_id=1, source_target_pairs={{0,14},{1,15},{2,0},{3,1},{4,2},{5,3},{6,4},{7,5},{8,6},{9,7},{10,... | collective-permute-start | bytes 368648 | tf_op jit(solution)/shard_map/ppermute | solution.py:48
  134.5 19.2 %all-to-all-start.4 = ((bf16[16,128,256]{2,1,0:T(8,128)(2,1)}), bf16[16,128,256]{2,1,0:T(8,128)(2,1)S(1)}, u32[]{:S(2)}, u32[]{:S(2)}) async-start(bf16[16,128,256]{2,1,0:T(8,128)(2,1)} %broadcast_in_dim.8), calls=%async_computation.4 | async-start | bytes 2097152 | tf_op jit(solution)/shard_map/all_to_all | solution.py:36
  138.2 15.6 %copy-start.10 = (bf16[480,128]{1,0:T(8,128)(2,1)}, bf16[480,128]{1,0:T(8,128)(2,1)S(1)}, u32[]{:S(2)}) copy-start(bf16[480,128]{1,0:T(8,128)(2,1)S(1)} %collective-permute-done.9.refs_8_) | copy-start | bytes 368644
  138.2 5.0 %collective-permute-start.10 = (bf16[480,128]{1,0:T(8,128)(2,1)S(1)}, bf16[480,128]{1,0:T(8,128)(2,1)S(1)}, u32[]{:S(2)}, u32[]{:S(2)}) collective-permute-start(bf16[480,128]{1,0:T(8,128)(2,1)S(1)} %collective-permute-done.9.refs_8_), channel_id=1, source_target_pairs={{0,2},{1,3},{2,4},{3,5},{4,6},{5,7},{6,8},{7,9},{8,10},{9,11},{10,... | collective-permute-start | bytes 368648 | tf_op jit(solution)/shard_map/ppermute | solution.py:48
  138.3 15.5 %copy-start.12 = (bf16[480,128]{1,0:T(8,128)(2,1)}, bf16[480,128]{1,0:T(8,128)(2,1)S(1)}, u32[]{:S(2)}) copy-start(bf16[480,128]{1,0:T(8,128)(2,1)S(1)} %collective-permute-done.5.refs_1_) | copy-start | bytes 368644
  138.3 4.9 %collective-permute-start.6 = (bf16[480,128]{1,0:T(8,128)(2,1)S(1)}, bf16[480,128]{1,0:T(8,128)(2,1)S(1)}, u32[]{:S(2)}, u32[]{:S(2)}) collective-permute-start(bf16[480,128]{1,0:T(8,128)(2,1)S(1)} %collective-permute-done.5.refs_1_), channel_id=1, source_target_pairs={{0,14},{1,15},{2,0},{3,1},{4,2},{5,3},{6,4},{7,5},{8,6},{9,7},{10,... | collective-permute-start | bytes 368648 | tf_op jit(solution)/shard_map/ppermute | solution.py:48
  143.2 10.6 %copy-start.11 = (bf16[480,128]{1,0:T(8,128)(2,1)}, bf16[480,128]{1,0:T(8,128)(2,1)S(1)}, u32[]{:S(2)}) copy-start(bf16[480,128]{1,0:T(8,128)(2,1)S(1)} %collective-permute-done.10.refs_7_) | copy-start | bytes 368644
  143.2 5.2 %collective-permute-start.11 = (bf16[480,128]{1,0:T(8,128)(2,1)S(1)}, bf16[480,128]{1,0:T(8,128)(2,1)S(1)}, u32[]{:S(2)}, u32[]{:S(2)}) collective-permute-start(bf16[480,128]{1,0:T(8,128)(2,1)S(1)} %collective-permute-done.10.refs_7_), channel_id=1, source_target_pairs={{0,2},{1,3},{2,4},{3,5},{4,6},{5,7},{6,8},{7,9},{8,10},{9,11},{10,... | collective-permute-start | bytes 368648 | tf_op jit(solution)/shard_map/ppermute | solution.py:48
  143.2 10.6 %copy-start.13 = (bf16[480,128]{1,0:T(8,128)(2,1)}, bf16[480,128]{1,0:T(8,128)(2,1)S(1)}, u32[]{:S(2)}) copy-start(bf16[480,128]{1,0:T(8,128)(2,1)S(1)} %collective-permute-done.6.refs_2_) | copy-start | bytes 368644
  143.3 5.3 %collective-permute-start.7 = (bf16[480,128]{1,0:T(8,128)(2,1)S(1)}, bf16[480,128]{1,0:T(8,128)(2,1)S(1)}, u32[]{:S(2)}, u32[]{:S(2)}) collective-permute-start(bf16[480,128]{1,0:T(8,128)(2,1)S(1)} %collective-permute-done.6.refs_2_), channel_id=1, source_target_pairs={{0,14},{1,15},{2,0},{3,1},{4,2},{5,3},{6,4},{7,5},{8,6},{9,7},{10,... | collective-permute-start | bytes 368648 | tf_op jit(solution)/shard_map/ppermute | solution.py:48
  148.5 5.3 %copy-start.8 = (bf16[480,128]{1,0:T(8,128)(2,1)}, bf16[480,128]{1,0:T(8,128)(2,1)S(1)}, u32[]{:S(2)}) copy-start(bf16[480,128]{1,0:T(8,128)(2,1)S(1)} %collective-permute-done.11.refs_6_) | copy-start | bytes 368644
  148.5 5.3 %collective-permute-start.14 = (bf16[240,128]{1,0:T(8,128)(2,1)S(1)}, bf16[240,128]{1,0:T(8,128)(2,1)S(1)}, u32[]{:S(2)}, u32[]{:S(2)}) collective-permute-start(bf16[240,128]{1,0:T(8,128)(2,1)S(1)} %slice.86), channel_id=1, source_target_pairs={{0,2},{1,3},{2,4},{3,5},{4,6},{5,7},{6,8},{7,9},{8,10},{9,11},{10,... | collective-permute-start | bytes 184328 | tf_op jit(solution)/shard_map/ppermute | solution.py:50
  148.6 5.2 %copy-start.9 = (bf16[480,128]{1,0:T(8,128)(2,1)}, bf16[480,128]{1,0:T(8,128)(2,1)S(1)}, u32[]{:S(2)}) copy-start(bf16[480,128]{1,0:T(8,128)(2,1)S(1)} %collective-permute-done.7.refs_3_) | copy-start | bytes 368644
  148.6 4.7 %collective-permute-start.8 = (bf16[240,128]{1,0:T(8,128)(2,1)S(1)}, bf16[240,128]{1,0:T(8,128)(2,1)S(1)}, u32[]{:S(2)}, u32[]{:S(2)}) collective-permute-start(bf16[240,128]{1,0:T(8,128)(2,1)S(1)} %slice.80), channel_id=1, source_target_pairs={{0,14},{1,15},{2,0},{3,1},{4,2},{5,3},{6,4},{7,5},{8,6},{9,7},{10,... | collective-permute-start | bytes 184328 | tf_op jit(solution)/shard_map/ppermute | solution.py:50
  153.3 0.6 copy-start.14
  153.7 0.6 copy-start.15
  153.7 1.0 copy-start.5
  161.2 10.5 %collective-permute-start.15 = (f32[448,256]{1,0:T(8,128)}, f32[448,256]{1,0:T(8,128)S(1)}, u32[]{:S(2)}, u32[]{:S(2)}) collective-permute-start(f32[448,256]{1,0:T(8,128)} %get-tuple-element.23), channel_id=1, source_target_pairs={{0,1},{1,0},{2,3},{3,2},{4,5},{5,4},{6,7},{7,6},{8,9},{9,8},{10,11... | collective-permute-start | bytes 1376264 | tf_op jit(solution)/shard_map/ppermute | solution.py:296
  167.3 4.4 %collective-permute-start.16 = (f32[448,256]{1,0:T(8,128)}, f32[448,256]{1,0:T(8,128)S(1)}, u32[]{:S(2)}, u32[]{:S(2)}) collective-permute-start(f32[448,256]{1,0:T(8,128)} %get-tuple-element.24), channel_id=1, source_target_pairs={{0,1},{1,0},{2,3},{3,2},{4,5},{5,4},{6,7},{7,6},{8,9},{9,8},{10,11... | collective-permute-start | bytes 1376264 | tf_op jit(solution)/shard_map/ppermute | solution.py:296
  167.4 4.3 %collective-permute-start.17 = (f32[448,256]{1,0:T(8,128)}, f32[448,256]{1,0:T(8,128)S(1)}, u32[]{:S(2)}, u32[]{:S(2)}) collective-permute-start(f32[448,256]{1,0:T(8,128)} %get-tuple-element.25), channel_id=1, source_target_pairs={{0,1},{1,0},{2,3},{3,2},{4,5},{5,4},{6,7},{7,6},{8,9},{9,8},{10,11... | collective-permute-start | bytes 1376264 | tf_op jit(solution)/shard_map/ppermute | solution.py:296
  169.3 1.2 collective-permute-start.12
Sparse Core Ops, SparseCore 0:
  9.8 63.6 all-gather.4
  80.2 52.8 all-gather.6
where the time goes:
time: 183 us; the launch traced here: 182 us
  waiting for transfers between devices  60.6 us (33%)
  starting transfers between devices  48.2 us (26%)
  blocking collectives  20 us (11%)
  between operations  16.3 us (9%)
  local copies, waits for them, and re-layouts  10.8 us (6%)
  Pallas kernels  10.1 us (6%)
  matrix products  8.75 us (5%)
  other arithmetic  7.37 us (4%)
    all_to_all x1, blocking collectives, shards(): blocks = lax.all_to_all(parts, GROUP, 0, 0, tiled=True)  20 us
    all_gather x1, waiting for transfers between devices, shards(): lax.all_gather(projector, 'dp', axis=0, axis_index_groups=LINES)  18.3 us
    all_to_all x1, waiting for transfers between devices, shards(): outgrad_gathered = lax.all_to_all(copies, GROUP, 0, 0, tiled=True)  17 us
    all_to_all x3, waiting for transfers between devices, gather_group(): return lax.all_to_all(copies, GROUP, 0, 0, tiled=True)  16.5 us
    all_to_all x3, starting transfers between devices, gather_group(): return lax.all_to_all(copies, GROUP, 0, 0, tiled=True)  16.3 us
    ppermute x6, starting transfers between devices, ring(): up, down = (lax.ppermute(up, 'dp', RIGHT), lax.ppermute(down, 'dp', LEFT))  13 us
    ppermute x3, starting transfers between devices, shards(): theirs = [lax.ppermute(part, 'dp', SIBLING) for part in theirs]  6.62 us
    unnamed x42, local copies, waits for them, and re-layouts  6.56 us
  transfers between devices with their start and end apart: 24, of which 8 were waited for; matrix products, arithmetic and copies ran while one was open for 11% of the time, Pallas kernels for 2%

commit v1 on v0

--- a/solution.py
+++ b/solution.py
@@ -96,6 +96,11 @@
     for i in range(16):
         copies_ref[i, :tokens] = outgrad
         copies_ref[i, tokens:] = loss
+
+
+def copies_kernel(block_ref, copies_ref):
+    for i in range(copies_ref.shape[0]):
+        copies_ref[i] = block_ref[...]
 
 
 def hidden_kernel(tokens, blocks_ref, down_ref, out_ref):
@@ -266,8 +271,16 @@
             flops=2 * 128 * 448 * 4096, bytes_accessed=5 * 2**20, transcendentals=0
         ),
     )(outgrad_gathered, down_weight)
-    outgrad_moved, _ = lax.optimization_barrier((outgrad_moved, grad_hidden))
-    outgrad_swapped = gather_group(outgrad_moved)
+    moved_copies = pl.pallas_call(
+        copies_kernel,
+        out_shape=jax.ShapeDtypeStruct((16, tokens, width), jnp.bfloat16),
+        in_specs=[vmem],
+        out_specs=vmem,
+        compiler_params=pltpu.CompilerParams(vmem_limit_bytes=16 * 2**20),
+        cost_estimate=pl.CostEstimate(flops=0, bytes_accessed=2 * 2**20, transcendentals=0),
+    )(outgrad_moved)
+    moved_copies, _ = lax.optimization_barrier((moved_copies, grad_hidden))
+    outgrad_swapped = lax.all_to_all(moved_copies, GROUP, 0, 0, tiled=True)
     line = ring(grad_hidden)
     line_loss = jnp.stack([found[-1][1][units - found[-1][0] :] for found in line])
     line_loss = rows_of(line_loss, 0, tokens)

time: 183 us -> 182 us (level)
    all_to_all x0 -> x1, starting transfers between devices: none -> 3.65 us  [shards(): outgrad_swapped = lax.all_to_all(moved_copies, GROUP, 0, 0, tiled=True)]
    all_to_all x3 -> x2, starting transfers between devices: 16.3 us -> 12.6 us  [gather_group(): return lax.all_to_all(copies, GROUP, 0, 0, tiled=True)]
    all_to_all x3 -> x2, waiting for transfers between devices: 16.5 us -> 16.5 us  [gather_group(): return lax.all_to_all(copies, GROUP, 0, 0, tiled=True)]
  transfers between devices with their start and end apart: 24 -> 24, of which waited for: 8 -> 8; matrix products, arithmetic and copies ran while one was open for 11% -> 10% of each run, Pallas kernels for 2% -> 3%
where the time goes in v1:
time: 182 us; the launch traced here: 181 us
  waiting for transfers between devices  59.6 us (33%)
  starting transfers between devices  48.3 us (27%)
  blocking collectives  20 us (11%)
  between operations  16.3 us (9%)
  Pallas kernels  11.1 us (6%)
  local copies, waits for them, and re-layouts  9.71 us (5%)
  matrix products  8.75 us (5%)
  other arithmetic  7.37 us (4%)
    all_to_all x1, blocking collectives, shards(): blocks = lax.all_to_all(parts, GROUP, 0, 0, tiled=True)  20 us
    all_gather x1, waiting for transfers between devices, shards(): lax.all_gather(projector, 'dp', axis=0, axis_index_groups=LINES)  18.3 us
    all_to_all x2, waiting for transfers between devices, gather_group(): return lax.all_to_all(copies, GROUP, 0, 0, tiled=True)  16.5 us
    all_to_all x1, waiting for transfers between devices, shards(): outgrad_gathered = lax.all_to_all(copies, GROUP, 0, 0, tiled=True)  15.9 us
    ppermute x6, starting transfers between devices, ring(): up, down = (lax.ppermute(up, 'dp', RIGHT), lax.ppermute(down, 'dp', LEFT))  13 us
    all_to_all x2, starting transfers between devices, gather_group(): return lax.all_to_all(copies, GROUP, 0, 0, tiled=True)  12.6 us
    ppermute x3, starting transfers between devices, shards(): theirs = [lax.ppermute(part, 'dp', SIBLING) for part in theirs]  6.62 us
    unnamed x42, local copies, waits for them, and re-layouts  6.56 us
  transfers between devices with their start and end apart: 24, of which 8 were waited for; matrix products, arithmetic and copies ran while one was open for 10% of the time, Pallas kernels for 3%

profile of v1, /device:TPU:1, one launch (start us, length us, event | category | flops | bytes accessed | tf_op | source)
XLA Modules:
  0.0 181.1 jit_solution(6311951196308925045)
XLA Ops:
  7.2 0.7 all-gather.5.cloned.1.call-update
  7.9 1.1 multiply_reduce_fusion
  9.1 0.8 pad_maximum_fusion.3
  9.9 1.1 broadcast_in_dim.4
  11.0 7.6 %all-to-all-start = ((bf16[16,144,256]{2,1,0:T(8,128)(2,1)}), bf16[16,144,256]{2,1,0:T(8,128)(2,1)S(1)}, u32[]{:S(2)}, u32[]{:S(2)}) async-start(bf16[16,144,256]{2,1,0:T(8,128)(2,1)} %broadcast_in_dim.4), calls=%async_computation | async-start | bytes 2359296 | tf_op jit(solution)/shard_map/all_to_all | solution.py:36
  18.6 0.7 collective-permute-start.4
  19.3 1.0 collective-permute-start.1
  20.4 16.5 %all-to-all-done = bf16[16,144,256]{2,1,0:T(8,128)(2,1)S(1)} async-done(((bf16[16,144,256]{2,1,0:T(8,128)(2,1)}), bf16[16,144,256]{2,1,0:T(8,128)(2,1)S(1)}, u32[]{:S(2)}, u32[]{:S(2)}) %all-to-all-start) | async-done | bytes 1179680 | tf_op jit(solution)/shard_map/all_to_all | solution.py:36
  37.0 0.7 copy.15
  37.7 2.6 %collective-permute-start.2 = (f32[128]{0:T(128)S(1)}, f32[128]{0:T(128)S(1)}, u32[]{:S(2)}, u32[]{:S(2)}) collective-permute-start(f32[128]{0:T(128)S(1)} %add_rsqrt_fusion), channel_id=1, source_target_pairs={{0,1},{1,0},{2,3},{3,2},{4,5},{5,4},{6,7},{7,6},{8,9},{9,8},{10,11... | collective-permute-start | bytes 1544 | tf_op jit(solution)/shard_map/ppermute | solution.py:214
  40.3 3.3 %convolution_bitcast_fusion.1 = f32[448,128]{1,0:T(8,128)S(1)} fusion(bf16[448,4096]{1,0:T(8,128)(2,1)} %param.9, bf16[128,4096]{0,1:T(8,128)(2,1)S(1)} %bitcast.74), kind=kOutput, calls=%fused_computation.3 | convolution fusion | flops 469762048 | bytes 4947968 | tf_op jit(solution)/shard_map/dot_general | solution.py:29
  43.6 1.8 %multiply_convert_fusion = (bf16[448,128]{1,0:T(8,128)(2,1)S(1)}, f32[448,128]{1,0:T(8,128)}) fusion(f32[448,128]{1,0:T(8,128)S(1)} %convolution_bitcast_fusion.1, bf16[448,4096]{1,0:T(8,128)(2,1)S(1)} %copy-done.16, bf16[128,4096]{0,1:T(8,128)(2,1)S(1)} %bitcast.75), kind=kOutput, calls=%fused_computation.17 | convolution fusion | flops 470106112 | bytes 5292032 | tf_op jit(solution)/shard_map/dot_general | solution.py:29
  45.5 1.1 broadcast_in_dim.5
  46.6 5.0 %all-to-all-start.1 = ((bf16[16,128,256]{2,1,0:T(8,128)(2,1)}), bf16[16,128,256]{2,1,0:T(8,128)(2,1)}, u32[]{:S(2)}, u32[]{:S(2)}) async-start(bf16[16,128,256]{2,1,0:T(8,128)(2,1)} %broadcast_in_dim.5), calls=%async_computation.1 | async-start | bytes 2097152 | tf_op jit(solution)/shard_map/all_to_all | solution.py:36
  51.8 2.1 %copy-done = bf16[448,4096]{1,0:T(8,128)(2,1)S(1)} copy-done((bf16[448,4096]{1,0:T(8,128)(2,1)S(1)}, bf16[448,4096]{1,0:T(8,128)(2,1)}, u32[]{:S(2)}) %copy-start) | copy-done | bytes 3670040
  53.9 1.3 shard_map.93
  55.2 18.3 %all-gather.5.cloned.1.call-done = bf16[8192,256]{1,0:T(8,128)(2,1)} async-done(((bf16[1024,256]{1,0:T(8,128)(2,1)}), bf16[8192,256]{1,0:T(8,128)(2,1)}) %all-gather.5.cloned.1.call-update) | async-done | bytes 4194320 | tf_op jit(solution)/shard_map/all_gather | solution.py:201
  73.5 3.6 %fusion.1 = f32[256,8,256]{2,0,1:T(8,128)S(1)} fusion(bf16[8,1024,256]{2,1,0:T(8,128)(2,1)} %bitcast.77, bf16[128,1024]{1,0:T(8,128)(2,1)} %collective-permute-done.1, bf16[128,1024]{1,0:T(8,128)(2,1)} %param.7), kind=kOutput, calls=%fused_computation.6 | convolution fusion | flops 1074790400 | bytes 6815744 | tf_op jit(solution)/shard_map/tk,zkn->ztn/dot_general | solution.py:232
  77.5 0.5 collective-permute-start.3
  78.1 1.7 pad_maximum_fusion.1
  80.1 20.0 %all_to_all.25.blocks_ref = bf16[16,128,256]{2,1,0:T(8,128)(2,1)S(1)} all-to-all(bf16[16,128,256]{2,1,0:T(8,128)(2,1)S(1)} %bitcast.73), channel_id=1, replica_groups=mesh['sec'=2,'tp'=8,'dp'=16] {'sec','tp'}, dimensions={0} | all-to-all | bytes 2097152 | tf_op jit(solution)/shard_map/all_to_all | solution.py:247
  100.1 1.2 shard_map.94
  101.3 3.7 %all-to-all-start.3 = ((bf16[16,144,256]{2,1,0:T(8,128)(2,1)}), bf16[16,144,256]{2,1,0:T(8,128)(2,1)S(1)}, u32[]{:S(2)}, u32[]{:S(2)}) async-start(bf16[16,144,256]{2,1,0:T(8,128)(2,1)} %get-tuple-element.17), calls=%async_computation.3 | async-start | bytes 2359296 | tf_op jit(solution)/shard_map/all_to_all | solution.py:261
  105.0 0.7 collective-permute-start.13
  105.7 1.0 shard_map.96
  106.8 15.9 %all-to-all-done.3.blocks_ref = bf16[16,144,256]{2,1,0:T(8,128)(2,1)S(1)} async-done(((bf16[16,144,256]{2,1,0:T(8,128)(2,1)}), bf16[16,144,256]{2,1,0:T(8,128)(2,1)S(1)}, u32[]{:S(2)}, u32[]{:S(2)}) %all-to-all-start.3) | async-done | bytes 1179680 | tf_op jit(solution)/shard_map/all_to_all | solution.py:261
  122.7 2.1 %copy-done.1 = bf16[448,4096]{1,0:T(8,128)(2,1)S(1)} copy-done((bf16[448,4096]{1,0:T(8,128)(2,1)S(1)}, bf16[448,4096]{1,0:T(8,128)(2,1)}, u32[]{:S(2)}) %copy-start.1) | copy-done | bytes 3670040
  124.8 1.1 shard_map.95.refs_0_
  125.9 3.7 %collective-permute-start.9 = (bf16[480,128]{1,0:T(8,128)(2,1)S(1)}, bf16[480,128]{1,0:T(8,128)(2,1)S(1)}, u32[]{:S(2)}, u32[]{:S(2)}) collective-permute-start(bf16[480,128]{1,0:T(8,128)(2,1)S(1)} %shard_map.95.refs_0_), channel_id=1, source_target_pairs={{0,2},{1,3},{2,4},{3,5},{4,6},{5,7},{6,8},{7,9},{8,10},{9,11},{10,... | collective-permute-start | bytes 368648 | tf_op jit(solution)/shard_map/ppermute | solution.py:48
  129.6 3.8 %collective-permute-start.5 = (bf16[480,128]{1,0:T(8,128)(2,1)S(1)}, bf16[480,128]{1,0:T(8,128)(2,1)S(1)}, u32[]{:S(2)}, u32[]{:S(2)}) collective-permute-start(bf16[480,128]{1,0:T(8,128)(2,1)S(1)} %shard_map.95.refs_0_), channel_id=1, source_target_pairs={{0,14},{1,15},{2,0},{3,1},{4,2},{5,3},{6,4},{7,5},{8,6},{9,7},{10,... | collective-permute-start | bytes 368648 | tf_op jit(solution)/shard_map/ppermute | solution.py:48
  133.4 3.7 %all-to-all-start.4 = ((bf16[16,128,256]{2,1,0:T(8,128)(2,1)}), bf16[16,128,256]{2,1,0:T(8,128)(2,1)S(1)}, u32[]{:S(2)}, u32[]{:S(2)}) async-start(bf16[16,128,256]{2,1,0:T(8,128)(2,1)} %shard_map.96), calls=%async_computation.4 | async-start | bytes 2097152 | tf_op jit(solution)/shard_map/all_to_all | solution.py:283
  137.3 2.6 %collective-permute-start.6 = (bf16[480,128]{1,0:T(8,128)(2,1)S(1)}, bf16[480,128]{1,0:T(8,128)(2,1)S(1)}, u32[]{:S(2)}, u32[]{:S(2)}) collective-permute-start(bf16[480,128]{1,0:T(8,128)(2,1)S(1)} %collective-permute-done.5.refs_1_), channel_id=1, source_target_pairs={{0,14},{1,15},{2,0},{3,1},{4,2},{5,3},{6,4},{7,5},{8,6},{9,7},{10,... | collective-permute-start | bytes 368648 | tf_op jit(solution)/shard_map/ppermute | solution.py:48
  139.9 2.2 %collective-permute-done.10.refs_7_ = bf16[480,128]{1,0:T(8,128)(2,1)S(1)} collective-permute-done((bf16[480,128]{1,0:T(8,128)(2,1)S(1)}, bf16[480,128]{1,0:T(8,128)(2,1)S(1)}, u32[]{:S(2)}, u32[]{:S(2)}) %collective-permute-start.10) | collective-permute-done | bytes 122912 | tf_op jit(solution)/shard_map/ppermute | solution.py:48
  142.2 2.7 %collective-permute-start.7 = (bf16[480,128]{1,0:T(8,128)(2,1)S(1)}, bf16[480,128]{1,0:T(8,128)(2,1)S(1)}, u32[]{:S(2)}, u32[]{:S(2)}) collective-permute-start(bf16[480,128]{1,0:T(8,128)(2,1)S(1)} %collective-permute-done.6.refs_2_), channel_id=1, source_target_pairs={{0,14},{1,15},{2,0},{3,1},{4,2},{5,3},{6,4},{7,5},{8,6},{9,7},{10,... | collective-permute-start | bytes 368648 | tf_op jit(solution)/shard_map/ppermute | solution.py:48
  144.9 2.5 %collective-permute-done.11.refs_6_ = bf16[480,128]{1,0:T(8,128)(2,1)S(1)} collective-permute-done((bf16[480,128]{1,0:T(8,128)(2,1)S(1)}, bf16[480,128]{1,0:T(8,128)(2,1)S(1)}, u32[]{:S(2)}, u32[]{:S(2)}) %collective-permute-start.11) | collective-permute-done | bytes 122912 | tf_op jit(solution)/shard_map/ppermute | solution.py:48
  147.5 2.8 %collective-permute-start.8 = (bf16[240,128]{1,0:T(8,128)(2,1)S(1)}, bf16[240,128]{1,0:T(8,128)(2,1)S(1)}, u32[]{:S(2)}, u32[]{:S(2)}) collective-permute-start(bf16[240,128]{1,0:T(8,128)(2,1)S(1)} %slice.80), channel_id=1, source_target_pairs={{0,14},{1,15},{2,0},{3,1},{4,2},{5,3},{6,4},{7,5},{8,6},{9,7},{10,... | collective-permute-start | bytes 184328 | tf_op jit(solution)/shard_map/ppermute | solution.py:50
  150.4 1.8 %collective-permute-done.8.refs_5_ = bf16[240,128]{1,0:T(8,128)(2,1)S(1)} collective-permute-done((bf16[240,128]{1,0:T(8,128)(2,1)S(1)}, bf16[240,128]{1,0:T(8,128)(2,1)S(1)}, u32[]{:S(2)}, u32[]{:S(2)}) %collective-permute-start.8) | collective-permute-done | bytes 61472 | tf_op jit(solution)/shard_map/ppermute | solution.py:50
  152.2 0.4 collective-permute-done.14.refs_4_
  152.8 0.5 copy-done.15
  153.3 0.4 copy-done.5
  153.6 6.5 %shard_map.97 = (f32[448,256]{1,0:T(8,128)}, f32[448,256]{1,0:T(8,128)}, f32[448,256]{1,0:T(8,128)}, f32[3,448,256]{2,1,0:T(8,128)}) custom-call(s32[2]{0:T(128)} %copy-done.4, f32[8,896,128]{2,1,0:T(8,128)} %bitcast.76, bf16[16,128,256]{2,1,0:T(8,128)(2,1)} %all-to-all-done.1.inputs_hbm, bf16[16,128,256]{2,1,0:T(8,128)(2,1)} %copy-done.5, ...), custom_call_target="tpu_custom_call" | custom-call | flops 1409286144 | bytes 10485760 | tf_op jit(solution)/shard_map/pallas_call | solution.py:291
  160.2 6.1 %collective-permute-start.15 = (f32[448,256]{1,0:T(8,128)}, f32[448,256]{1,0:T(8,128)S(1)}, u32[]{:S(2)}, u32[]{:S(2)}) collective-permute-start(f32[448,256]{1,0:T(8,128)} %get-tuple-element.23), channel_id=1, source_target_pairs={{0,1},{1,0},{2,3},{3,2},{4,5},{5,4},{6,7},{7,6},{8,9},{9,8},{10,11... | collective-permute-start | bytes 1376264 | tf_op jit(solution)/shard_map/ppermute | solution.py:309
  166.4 0.4 collective-permute-start.17
  166.8 0.7 constant_dynamic-update-slice_fusion.1
  167.5 0.7 constant_dynamic-update-slice_fusion
  168.4 1.0 collective-permute-done.12
  169.4 0.6 add_reduce_fusion
  170.7 2.4 %bitcast_add_fusion = (f32[448,256]{1,0:T(8,128)}, f32[448,256]{1,0:T(8,128)}, f32[448,256]{1,0:T(8,128)}) fusion(f32[448,256]{1,0:T(8,128)S(1)} %collective-permute-done.17, f32[3,448,256]{2,1,0:T(8,128)} %get-tuple-element.22, f32[448,256]{1,0:T(8,128)S(1)} %collective-permute-done.16, f32[448,256]{1,0:T(8,128)S(1)} %collective-permute-done.15), kind=kLoop, calls=%fused_computation.13 | loop fusion | flops 344064 | bytes 4128768 | tf_op jit(solution)/shard_map/add | solution.py:310
  (77 shorter events, 1.7 us)
Async XLA Ops:
  7.2 66.4 %all-gather.5.cloned.1.call-start = ((), (), s32[]{:S(2)}) async-start(), calls=%async_computation.5 | async-start | bytes 4718592 | tf_op jit(solution)/shard_map/all_gather | solution.py:201
  7.9 10.7 %copy-start.3 = (bf16[128,256]{1,0:T(8,128)(2,1)S(1)}, bf16[128,256]{1,0:T(8,128)(2,1)}, u32[]{:S(2)}) copy-start(bf16[128,256]{1,0:T(8,128)(2,1)} %inputs_ref.1) | copy-start | bytes 196612
  11.0 25.8 %all-to-all-start = ((bf16[16,144,256]{2,1,0:T(8,128)(2,1)}), bf16[16,144,256]{2,1,0:T(8,128)(2,1)S(1)}, u32[]{:S(2)}, u32[]{:S(2)}) async-start(bf16[16,144,256]{2,1,0:T(8,128)(2,1)} %broadcast_in_dim.4), calls=%async_computation | async-start | bytes 2359296 | tf_op jit(solution)/shard_map/all_to_all | solution.py:36
  18.6 26.9 %collective-permute-start.4 = (bf16[128,256]{1,0:T(8,128)(2,1)S(1)}, bf16[128,256]{1,0:T(8,128)(2,1)S(1)}, u32[]{:S(2)}, u32[]{:S(2)}) collective-permute-start(bf16[128,256]{1,0:T(8,128)(2,1)S(1)} %copy-done.3), channel_id=1, source_target_pairs={{0,0},{1,1},{2,32},{3,33},{4,64},{5,65},{6,96},{7,97},{8,128},{9,1... | collective-permute-start | bytes 196616 | tf_op jit(solution)/shard_map/ppermute | solution.py:202
  19.3 35.9 %collective-permute-start.1 = (bf16[128,1024]{1,0:T(8,128)(2,1)}, bf16[128,1024]{1,0:T(8,128)(2,1)}, u32[]{:S(2)}, u32[]{:S(2)}) collective-permute-start(bf16[128,1024]{1,0:T(8,128)(2,1)} %param.7), channel_id=1, source_target_pairs={{0,1},{1,0},{2,3},{3,2},{4,5},{5,4},{6,7},{7,6},{8,9},{9,8},{10,11... | collective-permute-start | bytes 786440 | tf_op jit(solution)/shard_map/ppermute | solution.py:204
  37.7 14.0 %collective-permute-start.2 = (f32[128]{0:T(128)S(1)}, f32[128]{0:T(128)S(1)}, u32[]{:S(2)}, u32[]{:S(2)}) collective-permute-start(f32[128]{0:T(128)S(1)} %add_rsqrt_fusion), channel_id=1, source_target_pairs={{0,1},{1,0},{2,3},{3,2},{4,5},{5,4},{6,7},{7,6},{8,9},{9,8},{10,11... | collective-permute-start | bytes 1544 | tf_op jit(solution)/shard_map/ppermute | solution.py:214
  40.3 3.3 %copy-start.16 = (bf16[448,4096]{1,0:T(8,128)(2,1)S(1)}, bf16[448,4096]{1,0:T(8,128)(2,1)}, u32[]{:S(2)}) copy-start(bf16[448,4096]{1,0:T(8,128)(2,1)} %param.10) | copy-start | bytes 11010052
  43.6 1.8 %copy-start.6 = (f32[448,128]{1,0:T(8,128)}, f32[448,128]{1,0:T(8,128)S(1)}, u32[]{:S(2)}) copy-start(f32[448,128]{1,0:T(8,128)S(1)} %convolution_bitcast_fusion.1) | copy-start | bytes 688132
  45.4 6.3 %collective-permute-start = (bf16[448,128]{1,0:T(8,128)(2,1)S(1)}, bf16[448,128]{1,0:T(8,128)(2,1)S(1)}, u32[]{:S(2)}, u32[]{:S(2)}) collective-permute-start(bf16[448,128]{1,0:T(8,128)(2,1)S(1)} %get-tuple-element.34), channel_id=1, source_target_pairs={{0,1},{1,0},{2,3},{3,2},{4,5},{5,4},{6,7},{7,6},{8,9},{9,8},{10,11... | collective-permute-start | bytes 344072 | tf_op jit(solution)/shard_map/ppermute | solution.py:220
  45.5 9.6 %copy-start.4 = (s32[2]{0:T(128)}, s32[2]{0:T(128)S(1)}, u32[]{:S(2)}) copy-start(s32[2]{0:T(128)S(1)} %pad_add_fusion.place_ref) | copy-start | bytes 28
  46.6 33.5 %all-to-all-start.1 = ((bf16[16,128,256]{2,1,0:T(8,128)(2,1)}), bf16[16,128,256]{2,1,0:T(8,128)(2,1)}, u32[]{:S(2)}, u32[]{:S(2)}) async-start(bf16[16,128,256]{2,1,0:T(8,128)(2,1)} %broadcast_in_dim.5), calls=%async_computation.1 | async-start | bytes 2097152 | tf_op jit(solution)/shard_map/all_to_all | solution.py:36
  51.6 101.0 %all-gather.7.cloned.1.call-start = ((), (), s32[]{:S(2)}) async-start(), calls=%async_computation.6 | async-start | bytes 4128768 | tf_op jit(solution)/shard_map/all_gather | solution.py:246
  51.8 2.1 %copy-start = (bf16[448,4096]{1,0:T(8,128)(2,1)S(1)}, bf16[448,4096]{1,0:T(8,128)(2,1)}, u32[]{:S(2)}) copy-start(bf16[448,4096]{1,0:T(8,128)(2,1)} %down_ref.3) | copy-start | bytes 11010052
  77.1 0.9 copy-start.7
  77.5 2.3 %collective-permute-start.3 = (bf16[8,128,256]{2,1,0:T(8,128)(2,1)S(1)}, bf16[8,128,256]{2,1,0:T(8,128)(2,1)S(1)}, u32[]{:S(2)}, u32[]{:S(2)}) collective-permute-start(bf16[8,128,256]{2,1,0:T(8,128)(2,1)S(1)} %slice.75), channel_id=1, source_target_pairs={{0,1},{1,0},{2,3},{3,2},{4,5},{5,4},{6,7},{7,6},{8,9},{9,8},{10,11... | collective-permute-start | bytes 1572872 | tf_op jit(solution)/shard_map/ppermute | solution.py:240
  101.3 21.4 %all-to-all-start.3 = ((bf16[16,144,256]{2,1,0:T(8,128)(2,1)}), bf16[16,144,256]{2,1,0:T(8,128)(2,1)S(1)}, u32[]{:S(2)}, u32[]{:S(2)}) async-start(bf16[16,144,256]{2,1,0:T(8,128)(2,1)} %get-tuple-element.17), calls=%async_computation.3 | async-start | bytes 2359296 | tf_op jit(solution)/shard_map/all_to_all | solution.py:261
  105.0 0.7 collective-permute-start.13
  122.7 2.1 %copy-start.1 = (bf16[448,4096]{1,0:T(8,128)(2,1)S(1)}, bf16[448,4096]{1,0:T(8,128)(2,1)}, u32[]{:S(2)}) copy-start(bf16[448,4096]{1,0:T(8,128)(2,1)} %down_ref.3) | copy-start | bytes 11010052
  125.9 26.8 %copy-start.2 = (bf16[480,128]{1,0:T(8,128)(2,1)}, bf16[480,128]{1,0:T(8,128)(2,1)S(1)}, u32[]{:S(2)}) copy-start(bf16[480,128]{1,0:T(8,128)(2,1)S(1)} %shard_map.95.refs_0_) | copy-start | bytes 368644
  125.9 11.2 %collective-permute-start.9 = (bf16[480,128]{1,0:T(8,128)(2,1)S(1)}, bf16[480,128]{1,0:T(8,128)(2,1)S(1)}, u32[]{:S(2)}, u32[]{:S(2)}) collective-permute-start(bf16[480,128]{1,0:T(8,128)(2,1)S(1)} %shard_map.95.refs_0_), channel_id=1, source_target_pairs={{0,2},{1,3},{2,4},{3,5},{4,6},{5,7},{6,8},{7,9},{8,10},{9,11},{10,... | collective-permute-start | bytes 368648 | tf_op jit(solution)/shard_map/ppermute | solution.py:48
  129.6 7.6 %collective-permute-start.5 = (bf16[480,128]{1,0:T(8,128)(2,1)S(1)}, bf16[480,128]{1,0:T(8,128)(2,1)S(1)}, u32[]{:S(2)}, u32[]{:S(2)}) collective-permute-start(bf16[480,128]{1,0:T(8,128)(2,1)S(1)} %shard_map.95.refs_0_), channel_id=1, source_target_pairs={{0,14},{1,15},{2,0},{3,1},{4,2},{5,3},{6,4},{7,5},{8,6},{9,7},{10,... | collective-permute-start | bytes 368648 | tf_op jit(solution)/shard_map/ppermute | solution.py:48
  133.4 19.2 %all-to-all-start.4 = ((bf16[16,128,256]{2,1,0:T(8,128)(2,1)}), bf16[16,128,256]{2,1,0:T(8,128)(2,1)S(1)}, u32[]{:S(2)}, u32[]{:S(2)}) async-start(bf16[16,128,256]{2,1,0:T(8,128)(2,1)} %shard_map.96), calls=%async_computation.4 | async-start | bytes 2097152 | tf_op jit(solution)/shard_map/all_to_all | solution.py:283
  137.1 15.6 %copy-start.10 = (bf16[480,128]{1,0:T(8,128)(2,1)}, bf16[480,128]{1,0:T(8,128)(2,1)S(1)}, u32[]{:S(2)}) copy-start(bf16[480,128]{1,0:T(8,128)(2,1)S(1)} %collective-permute-done.9.refs_8_) | copy-start | bytes 368644
  137.1 5.0 %collective-permute-start.10 = (bf16[480,128]{1,0:T(8,128)(2,1)S(1)}, bf16[480,128]{1,0:T(8,128)(2,1)S(1)}, u32[]{:S(2)}, u32[]{:S(2)}) collective-permute-start(bf16[480,128]{1,0:T(8,128)(2,1)S(1)} %collective-permute-done.9.refs_8_), channel_id=1, source_target_pairs={{0,2},{1,3},{2,4},{3,5},{4,6},{5,7},{6,8},{7,9},{8,10},{9,11},{10,... | collective-permute-start | bytes 368648 | tf_op jit(solution)/shard_map/ppermute | solution.py:48
  137.2 15.5 %copy-start.12 = (bf16[480,128]{1,0:T(8,128)(2,1)}, bf16[480,128]{1,0:T(8,128)(2,1)S(1)}, u32[]{:S(2)}) copy-start(bf16[480,128]{1,0:T(8,128)(2,1)S(1)} %collective-permute-done.5.refs_1_) | copy-start | bytes 368644
  137.3 4.9 %collective-permute-start.6 = (bf16[480,128]{1,0:T(8,128)(2,1)S(1)}, bf16[480,128]{1,0:T(8,128)(2,1)S(1)}, u32[]{:S(2)}, u32[]{:S(2)}) collective-permute-start(bf16[480,128]{1,0:T(8,128)(2,1)S(1)} %collective-permute-done.5.refs_1_), channel_id=1, source_target_pairs={{0,14},{1,15},{2,0},{3,1},{4,2},{5,3},{6,4},{7,5},{8,6},{9,7},{10,... | collective-permute-start | bytes 368648 | tf_op jit(solution)/shard_map/ppermute | solution.py:48
  142.2 10.6 %copy-start.11 = (bf16[480,128]{1,0:T(8,128)(2,1)}, bf16[480,128]{1,0:T(8,128)(2,1)S(1)}, u32[]{:S(2)}) copy-start(bf16[480,128]{1,0:T(8,128)(2,1)S(1)} %collective-permute-done.10.refs_7_) | copy-start | bytes 368644
  142.2 5.2 %collective-permute-start.11 = (bf16[480,128]{1,0:T(8,128)(2,1)S(1)}, bf16[480,128]{1,0:T(8,128)(2,1)S(1)}, u32[]{:S(2)}, u32[]{:S(2)}) collective-permute-start(bf16[480,128]{1,0:T(8,128)(2,1)S(1)} %collective-permute-done.10.refs_7_), channel_id=1, source_target_pairs={{0,2},{1,3},{2,4},{3,5},{4,6},{5,7},{6,8},{7,9},{8,10},{9,11},{10,... | collective-permute-start | bytes 368648 | tf_op jit(solution)/shard_map/ppermute | solution.py:48
  142.2 10.6 %copy-start.13 = (bf16[480,128]{1,0:T(8,128)(2,1)}, bf16[480,128]{1,0:T(8,128)(2,1)S(1)}, u32[]{:S(2)}) copy-start(bf16[480,128]{1,0:T(8,128)(2,1)S(1)} %collective-permute-done.6.refs_2_) | copy-start | bytes 368644
  142.2 5.3 %collective-permute-start.7 = (bf16[480,128]{1,0:T(8,128)(2,1)S(1)}, bf16[480,128]{1,0:T(8,128)(2,1)S(1)}, u32[]{:S(2)}, u32[]{:S(2)}) collective-permute-start(bf16[480,128]{1,0:T(8,128)(2,1)S(1)} %collective-permute-done.6.refs_2_), channel_id=1, source_target_pairs={{0,14},{1,15},{2,0},{3,1},{4,2},{5,3},{6,4},{7,5},{8,6},{9,7},{10,... | collective-permute-start | bytes 368648 | tf_op jit(solution)/shard_map/ppermute | solution.py:48
  147.4 5.3 %copy-start.8 = (bf16[480,128]{1,0:T(8,128)(2,1)}, bf16[480,128]{1,0:T(8,128)(2,1)S(1)}, u32[]{:S(2)}) copy-start(bf16[480,128]{1,0:T(8,128)(2,1)S(1)} %collective-permute-done.11.refs_6_) | copy-start | bytes 368644
  147.4 5.3 %collective-permute-start.14 = (bf16[240,128]{1,0:T(8,128)(2,1)S(1)}, bf16[240,128]{1,0:T(8,128)(2,1)S(1)}, u32[]{:S(2)}, u32[]{:S(2)}) collective-permute-start(bf16[240,128]{1,0:T(8,128)(2,1)S(1)} %slice.86), channel_id=1, source_target_pairs={{0,2},{1,3},{2,4},{3,5},{4,6},{5,7},{6,8},{7,9},{8,10},{9,11},{10,... | collective-permute-start | bytes 184328 | tf_op jit(solution)/shard_map/ppermute | solution.py:50
  147.5 5.2 %copy-start.9 = (bf16[480,128]{1,0:T(8,128)(2,1)}, bf16[480,128]{1,0:T(8,128)(2,1)S(1)}, u32[]{:S(2)}) copy-start(bf16[480,128]{1,0:T(8,128)(2,1)S(1)} %collective-permute-done.7.refs_3_) | copy-start | bytes 368644
  147.5 4.7 %collective-permute-start.8 = (bf16[240,128]{1,0:T(8,128)(2,1)S(1)}, bf16[240,128]{1,0:T(8,128)(2,1)S(1)}, u32[]{:S(2)}, u32[]{:S(2)}) collective-permute-start(bf16[240,128]{1,0:T(8,128)(2,1)S(1)} %slice.80), channel_id=1, source_target_pairs={{0,14},{1,15},{2,0},{3,1},{4,2},{5,3},{6,4},{7,5},{8,6},{9,7},{10,... | collective-permute-start | bytes 184328 | tf_op jit(solution)/shard_map/ppermute | solution.py:50
  152.2 0.6 copy-start.14
  152.7 0.6 copy-start.15
  152.7 1.0 copy-start.5
  160.2 10.5 %collective-permute-start.15 = (f32[448,256]{1,0:T(8,128)}, f32[448,256]{1,0:T(8,128)S(1)}, u32[]{:S(2)}, u32[]{:S(2)}) collective-permute-start(f32[448,256]{1,0:T(8,128)} %get-tuple-element.23), channel_id=1, source_target_pairs={{0,1},{1,0},{2,3},{3,2},{4,5},{5,4},{6,7},{7,6},{8,9},{9,8},{10,11... | collective-permute-start | bytes 1376264 | tf_op jit(solution)/shard_map/ppermute | solution.py:309
  166.3 4.4 %collective-permute-start.16 = (f32[448,256]{1,0:T(8,128)}, f32[448,256]{1,0:T(8,128)S(1)}, u32[]{:S(2)}, u32[]{:S(2)}) collective-permute-start(f32[448,256]{1,0:T(8,128)} %get-tuple-element.24), channel_id=1, source_target_pairs={{0,1},{1,0},{2,3},{3,2},{4,5},{5,4},{6,7},{7,6},{8,9},{9,8},{10,11... | collective-permute-start | bytes 1376264 | tf_op jit(solution)/shard_map/ppermute | solution.py:309
  166.4 4.3 %collective-permute-start.17 = (f32[448,256]{1,0:T(8,128)}, f32[448,256]{1,0:T(8,128)S(1)}, u32[]{:S(2)}, u32[]{:S(2)}) collective-permute-start(f32[448,256]{1,0:T(8,128)} %get-tuple-element.25), channel_id=1, source_target_pairs={{0,1},{1,0},{2,3},{3,2},{4,5},{5,4},{6,7},{7,6},{8,9},{9,8},{10,11... | collective-permute-start | bytes 1376264 | tf_op jit(solution)/shard_map/ppermute | solution.py:309
  168.2 1.2 collective-permute-start.12
Sparse Core Ops, SparseCore 0:
  9.8 63.6 all-gather.4
  80.2 52.8 all-gather.6
